TPU v7x, 32 devices: a whole 2x2x4 slice. The times are simulated.
32 devices in a mesh: dp: 8 (over z, x), tensor: 4 (over y, core).
Axes of the slice: x: 2, y: 2, z: 4, core: 2. Of those that a mesh axis runs over, the one named last changes fastest.
Arguments:
- tokens: bfloat16 [2048, 1536], P('dp'), may hold values from -6 to 6
- targets: bfloat16 [2048, 1536], P('dp'), may hold values from -6 to 6
- modulation: bfloat16 [16, 3, 1536], P('dp'), may hold values from -2.5 to 2.5
- live_block_count: int32 [8], P('dp'), may hold values from 2 to 4, as said below
- preferred_blocks: int32 [8], P('dp'), may hold values from 1 to 3, as said below
- last_block_rows: int32 [8, 2], P('dp'), may hold values from 1 to 64
- up_projection_weight: bfloat16 [1536, 6144], P('dp', 'tensor'), may hold values from -0.15625 to 0.15625
- down_weight_transposed: bfloat16 [1536, 6144], P('dp', 'tensor'), may hold values from -0.078125 to 0.078125
- adapter_input_factor: bfloat16 [1536, 64], replicated, may hold values from -0.15625 to 0.15625
- adapter_output_factor: bfloat16 [64, 6144], P(None, 'tensor'), may hold values from -0.75 to 0.75
Outputs:
- losses: float32 [8], P('dp')
- grad_tokens: bfloat16 [2048, 1536], P('dp')
- grad_lora_a: float32 [1536, 64], replicated
- grad_lora_b: float32 [64, 6144], P(None, 'tensor')
Inputs may be any that keep to these rules, and one draw needn't show every extreme that they name: `live_block_count`: device i of dp and device (i + 4) modulo 8 together hold 6 live blocks; some pair holds 4. `preferred_blocks`: at most live_block_count - 1 for each pair, so the loser has a block too.
All inputs are finite; a program needn't handle non-finite values.
Results may differ from a plain program's by a relative error of at most 0.035.
Values may be sent and summed in bfloat16 or wider, within the bound.
A program may use at most 64 MiB of HBM per device.

v0:
```python
import jax
import jax.numpy as jnp
from jax import lax
from jax.experimental import pallas as pl
from jax.experimental.pallas import tpu as pltpu
from jax.sharding import PartitionSpec as P

BLK = 64
CAP = 4


EPS = 1e-06
BETA = 20.0
LOSS_SCALE = 4096.0


def settle_gradients(value):
    return lax.optimization_barrier(value.astype(jnp.bfloat16)).astype(jnp.float32)


def layer_norm(image_blocks):
    wide = image_blocks.astype(jnp.float32)
    center = wide - jnp.mean(wide, axis=-1, keepdims=True)
    inverse_deviation = lax.rsqrt(jnp.mean(center * center, axis=-1, keepdims=True) + EPS)
    return (center * inverse_deviation, inverse_deviation)


def gelu_and_slope(pre):

    def act(value):
        return jax.nn.gelu(value, approximate=True)

    value, back = jax.vjp(act, pre)
    return (value, back(jnp.ones_like(pre))[0])


def contract_trailing(left, right):
    return lax.dot_general(
        left, right, (((1,), (1,)), ((), ())), preferred_element_type=jnp.float32
    )


def contract_first(left, right):
    return lax.dot_general(
        left, right, (((0,), (0,)), ((), ())), preferred_element_type=jnp.float32
    )


def slot_state(live_block_count, preferred_blocks, last_block_rows):
    count = live_block_count[0]
    wins = preferred_blocks[0]
    slots = jnp.arange(CAP, dtype=jnp.int32)
    flags = (slots >= wins).astype(jnp.int32)
    last = jnp.where(flags == 0, wins - 1, count - 1)
    tail = jnp.where(flags == 0, last_block_rows[0, 0], last_block_rows[0, 1])
    live = jnp.where(slots < count, jnp.where(slots == last, tail, BLK), 0)
    masks = (jnp.arange(BLK, dtype=jnp.int32)[None, :] < live[:, None]).astype(jnp.float32)
    own_counts = jnp.stack(
        [jnp.sum(jnp.where(flags == 0, live, 0)), jnp.sum(jnp.where(flags == 1, live, 0))]
    ).astype(jnp.float32)
    return flags, masks, own_counts


def per_device(
    tokens,
    targets,
    modulation,
    live_block_count,
    preferred_blocks,
    last_block_rows,
    up_projection_weight,
    down_weight_transposed,
    adapter_input_factor,
    adapter_output_factor,
):
    width = tokens.shape[1]
    n_dp = lax.axis_size("dp")
    here = lax.axis_index("dp")
    flags, masks, own_counts = slot_state(live_block_count, preferred_blocks, last_block_rows)
    blocks_x = tokens.reshape(CAP, BLK, width)
    blocks_t = targets.reshape(CAP, BLK, width)
    blocks_mod = jnp.where(flags[:, None, None] == 0, modulation[0][None], modulation[1][None])
    homes = jnp.full((CAP,), here, jnp.int32)
    work_x, work_t, work_mod = (blocks_x, blocks_t, blocks_mod)
    work_mask, work_flag, work_home = (masks, flags, homes)
    spots = work_x.shape[0]
    count_rows = spots * BLK
    samples = 2 * n_dp
    ids = work_home * 2 + work_flag
    picks = (ids[:, None] == jnp.arange(samples, dtype=jnp.int32)[None, :]).astype(jnp.float32)
    modulation_vectors = work_mod.astype(jnp.float32)
    shift = modulation_vectors[:, None, 0]
    modulation_scale = 1.0 + modulation_vectors[:, None, 1]
    output_gate = modulation_vectors[:, None, 2]
    normalized_input, inverse_deviation = layer_norm(work_x)
    modulated_input = (
        (normalized_input * modulation_scale + shift)
        .astype(jnp.bfloat16)
        .reshape(count_rows, width)
    )
    w_up, w_down = (
        lax.all_gather(up_projection_weight, "dp", axis=0, tiled=True),
        lax.all_gather(down_weight_transposed, "dp", axis=0, tiled=True),
    )
    low_rank_hidden = jnp.dot(
        modulated_input, adapter_input_factor, preferred_element_type=jnp.float32
    ).astype(jnp.bfloat16)
    reference_preactivation = jnp.dot(modulated_input, w_up, preferred_element_type=jnp.float32)
    policy_preactivation = reference_preactivation + jnp.dot(
        low_rank_hidden, adapter_output_factor, preferred_element_type=jnp.float32
    )
    act_pol, policy_activation_slope = gelu_and_slope(policy_preactivation)
    hid_pol = act_pol.astype(jnp.bfloat16)
    hid_ref = jax.nn.gelu(reference_preactivation, approximate=True).astype(jnp.bfloat16)
    part_pol = settle_gradients(contract_trailing(hid_pol, w_down))
    part_ref = settle_gradients(contract_trailing(hid_ref, w_down))
    sum_pol, sum_ref = (
        lax.psum(part_pol.astype(jnp.bfloat16), "tensor").astype(jnp.float32),
        lax.psum(part_ref.astype(jnp.bfloat16), "tensor").astype(jnp.float32),
    )
    x_part = work_x.astype(jnp.float32)
    t_part = work_t.astype(jnp.float32)
    wmask = work_mask[:, :, None]
    miss_pol = x_part + output_gate * sum_pol.reshape(spots, BLK, width) - t_part
    miss_ref = x_part + output_gate * sum_ref.reshape(spots, BLK, width) - t_part
    vec_pol = jnp.sum(jnp.sum(wmask * miss_pol * miss_pol, axis=(1, 2))[:, None] * picks, axis=0)
    vec_ref = jnp.sum(jnp.sum(wmask * miss_ref * miss_ref, axis=(1, 2))[:, None] * picks, axis=0)
    owned = (jnp.arange(samples, dtype=jnp.int32) // 2 == here).astype(jnp.float32) * jnp.tile(
        own_counts, n_dp
    )
    tot_pol, tot_ref, tot_rows = lax.psum((vec_pol, vec_ref, owned), "dp")
    scale_rows = 1.0 / (width * tot_rows)
    pair_gap = ((tot_pol - tot_ref) * scale_rows).reshape(n_dp, 2)
    inside = -BETA * (pair_gap[:, 0] - pair_gap[:, 1])
    losses = lax.dynamic_slice_in_dim(jax.nn.softplus(-inside), here, 1)
    weight = BETA * LOSS_SCALE * jax.nn.sigmoid(-inside)
    coef = jnp.stack([weight, -weight], axis=1).reshape(samples) * scale_rows
    slot_coef = jnp.sum(picks * coef[None, :], axis=1)
    out_grad = slot_coef[:, None, None] * 2.0 * wmask * miss_pol
    dy_part = (output_gate * out_grad).astype(jnp.bfloat16).reshape(count_rows, width)
    dh = jnp.dot(dy_part, w_down, preferred_element_type=jnp.float32)
    preactivation_gradient = (dh * policy_activation_slope).astype(jnp.bfloat16)
    grad_b = contract_first(low_rank_hidden, preactivation_gradient)
    low_rank_gradient_piece = settle_gradients(
        contract_trailing(preactivation_gradient, adapter_output_factor)
    )
    dm_part = settle_gradients(contract_trailing(preactivation_gradient, w_up))
    modulation_gradient_sum, dlow_sum = (
        lax.psum(dm_part.astype(jnp.bfloat16), "tensor").astype(jnp.float32),
        lax.psum(low_rank_gradient_piece.astype(jnp.bfloat16), "tensor").astype(jnp.float32),
    )
    low_rank_gradient = dlow_sum.astype(jnp.bfloat16)
    modulation_gradient = modulation_gradient_sum + contract_trailing(
        low_rank_gradient, adapter_input_factor
    )
    dn = modulation_gradient.reshape(spots, BLK, width) * modulation_scale
    first_sum = jnp.sum(dn, axis=-1, keepdims=True)
    second_sum = jnp.sum(dn * normalized_input, axis=-1, keepdims=True)
    back_part = inverse_deviation * (dn - first_sum / width - normalized_input * second_sum / width)
    grad_part = (out_grad + back_part).astype(jnp.bfloat16)
    grad_a = contract_first(modulated_input, low_rank_gradient)
    sum_a, sum_b = lax.psum((grad_a, grad_b), "dp")
    return (losses, grad_part.reshape(CAP * BLK, width), sum_a / n_dp, sum_b / n_dp)


MESH = pl.DeviceIdType.MESH
F32 = jnp.float32
BF16 = jnp.bfloat16
SIDE = 32
TILE = 384
PAD = 128
GELU_ROOT = 0.7978845608028654
GELU_CUBE = 0.044715


def activation(pre, want_slope):
    square = pre * pre
    bend = jnp.tanh(GELU_ROOT * pre * (1.0 + GELU_CUBE * square))
    half = 0.5 * (1.0 + bend)
    if not want_slope:
        return pre * half
    slope = half + 0.5 * pre * (1.0 - bend * bend) * GELU_ROOT * (1.0 + 3.0 * GELU_CUBE * square)
    return pre * half, slope


def step_kernel(
    live_ref, wins_ref, tail_ref, x_hbm, t_hbm, mod_hbm, up_ref, dn_ref, a_hbm, b_hbm,
    loss_ref, grad_out, ga_out, gb_out,
    x_ref, t_ref, mod_in, a_in, b_ref, at_ref, mod_ref, mask_ref, flag_ref,
    grad_ref, ga_ref, gb_ref, gat_wide, local,
    w_ref, modded, low_ref, lowt_ref, slope_ref, hid_ref,
    ypart, crecv, ysend, yrecv, ysum, miss_ref, vbuf, ebuf, cf_ref,
    dpre_ref, dmpart, dmc, dmsend, dmrecv, dmsum,
    dlpart, dlc, dlsend, dlrecv, dlsum,
    gat, gatr, gap, gapr, gbp, gbr,
    z_send, z_recv, x_send, x_recv, c_send, c_recv, y_send, y_recv, v_send, v_recv,
    e_send, e_recv, dc_send, dc_recv, dy_send, dy_recv, g_send, g_recv,
    at_send, at_recv, rs_send, rs_recv, ag_send, ag_recv, tg_send, tg_recv,
):
    d = lax.axis_index("dp")
    t = lax.axis_index("tensor")
    z, x = d // 2, d % 2
    y, core = t // 2, t % 2
    high = z // 2
    middle = (z + high) % 2
    base = [middle, 1 - middle, 2, 3]
    place = [p + high * (3 - 2 * p) for p in base]
    inner = ((z + 1 - 2 * high) * 2 + x, t)
    edge_z = z - 1 + 2 * high
    edge = ((edge_z * middle + (1 - middle) * (z + 1 - 2 * high)) * 2 + x, t)
    across = (z * 2 + 1 - x, t)
    t_core = y * 2 + 1 - core
    t_y = (1 - y) * 2 + core
    t_far = (1 - y) * 2 + 1 - core
    mate = (d, t_core)
    over = (d, t_y)
    far = (d, t_far)
    peers = [mate, over, far]
    is_middle = middle == 1

    barrier = pltpu.get_barrier_semaphore()
    for k in range(1, 8):
        pl.semaphore_signal(barrier, inc=1, device_id=((d + k) % 8, t), device_id_type=MESH)
    for peer in peers:
        pl.semaphore_signal(barrier, inc=1, device_id=peer, device_id_type=MESH)

    shard = up_ref.shape[0]
    main = shard - SIDE
    half = main // 2
    here = pl.ds(d * shard, shard)
    loads = [
        pltpu.make_async_copy(src, dst, local.at[k]) for k, (src, dst) in enumerate((
            (up_ref, w_ref.at[0, here, :]), (dn_ref, w_ref.at[1, here, :]),
            (x_hbm, x_ref), (mod_hbm, mod_in), (a_hbm, a_in),
            (b_hbm, b_ref.at[pl.ds(0, b_hbm.shape[0]), :]), (t_hbm, t_ref)))]
    for load in loads:
        load.start()
    loads[0].wait()
    loads[1].wait()
    pl.semaphore_wait(barrier, 10)

    def copy(src, dst, send, recv, device):
        return pltpu.make_async_remote_copy(
            src_ref=src, dst_ref=dst, send_sem=send, recv_sem=recv,
            device_id=device, device_id_type=MESH)

    def rows(m, kind, slot):
        column = 1 - x if kind == 2 else x
        start = (0, half, main)[kind]
        size = (half, shard - half, SIDE)[kind]
        return w_ref.at[m, pl.ds((place[slot] * 2 + column) * shard + start, size), :]

    def x_rows(m, piece, column):
        slot, part = (0, 2) if piece == 8 else (piece // 2, piece % 2)
        size = SIDE if part == 2 else half
        return w_ref.at[m, pl.ds((place[slot] * 2 + column) * shard + part * half, size), :]

    def z_copy(m, kind, which):
        slot = [0, 0, 1, 2, 3][which]
        target = [1 + middle, 1, 3, 2, 3][which]
        device = inner if which in (0, 2) else edge
        ref = rows(m, kind, slot)
        return copy(ref, ref, z_send.at[m, kind, which], z_recv.at[m, kind, target], device)

    def z_arrive(m, kind, slot):
        ref = rows(m, kind, slot)
        copy(ref, ref, z_send.at[m, kind, 0], z_recv.at[m, kind, slot], inner).wait_recv()

    def x_copy(m, piece):
        ref = x_rows(m, piece, x)
        return copy(ref, ref, x_send.at[m, piece], x_recv.at[m, piece], across)

    def x_arrive(m, piece):
        ref = x_rows(m, piece, 1 - x)
        copy(ref, ref, x_send.at[m, piece], x_recv.at[m, piece], across).wait_recv()

    def begin_inner(m):
        x_copy(m, 8).start()
        for part in range(2):
            z_copy(m, part, 0).start()
            x_copy(m, part).start()

    def begin_edge(m):
        @pl.when(is_middle)
        def _():
            for part in range(2):
                z_copy(m, part, 1).start()

    def side_begin(m):
        x_arrive(m, 8)
        z_copy(m, 2, 0).start()

        @pl.when(is_middle)
        def _():
            z_copy(m, 2, 1).start()

    def relay(m, slot):
        for part in range(2):
            z_arrive(m, part, slot)

            @pl.when(is_middle)
            def _():
                z_copy(m, part, slot + 1).start()

            x_copy(m, slot * 2 + part).start()

    def side_relay(m, slot):
        z_arrive(m, 2, slot)

        @pl.when(is_middle)
        def _():
            z_copy(m, 2, slot + 1).start()

    begin_edge(0)
    begin_inner(0)

    count, wins = live_ref[0], wins_ref[0]
    tail_w, tail_l = tail_ref[0, 0], tail_ref[0, 1]
    loser_here = t >= wins
    last = jnp.where(loser_here, count - 1, wins - 1)
    tail = jnp.where(loser_here, tail_l, tail_w)
    live = jnp.where(t < count, jnp.where(t == last, tail, BLK), 0)
    spot = lax.broadcasted_iota(jnp.int32, (BLK, 1), 0)
    mask_ref[...] = jnp.where(spot < live, 1.0, 0.0)
    line = lax.broadcasted_iota(jnp.int32, (8, PAD), 0)
    flag_ref[...] = jnp.where(line >= wins, 1.0, 0.0)
    width = x_ref.shape[1]
    rows_w = jnp.broadcast_to(((wins - 1) * BLK + tail_w).astype(F32), (1, PAD))
    rows_l = jnp.broadcast_to(((count - wins - 1) * BLK + tail_l).astype(F32), (1, PAD))
    for load in loads[2:]:
        load.wait()
    rank = a_in.shape[1]
    b_ref[rank:PAD, :] = jnp.zeros((PAD - rank, b_ref.shape[1]), BF16)
    a_wide = jnp.concatenate(
        [a_in[...].astype(F32), jnp.zeros((width, PAD - rank), F32)], axis=1)
    at_ref[...] = a_wide.T.astype(BF16)
    for b in range(CAP):
        loser = flag_ref[b:b + 1, 0:1]
        mod_ref[b] = (1.0 - loser) * mod_in[0].astype(F32) + loser * mod_in[1].astype(F32)

    def norm(block, b):
        wide = x_ref[block, :].astype(F32)
        center = wide - jnp.mean(wide, axis=-1, keepdims=True)
        inverse = lax.rsqrt(jnp.mean(center * center, axis=-1, keepdims=True) + EPS)
        vectors = mod_ref[b]
        return wide, center * inverse, inverse, vectors[0:1], 1.0 + vectors[1:2], vectors[2:3]

    @pl.loop(0, CAP)
    def _(b):
        block = pl.ds(b * BLK, BLK)
        _, normed, _, shift, scale, _ = norm(block, b)
        modded[block, :] = (normed * scale + shift).astype(BF16)

    low_ref[...] = contract_trailing(modded[...], at_ref[...]).astype(BF16)
    lowt_ref[...] = contract_trailing(at_ref[...], modded[...]).astype(BF16)

    side_begin(0)
    relay(0, 1)
    begin_inner(1)
    side_relay(0, 1)
    relay(0, 2)
    side_relay(0, 2)
    relay(0, 3)
    side_relay(0, 3)
    begin_edge(1)
    side_begin(1)

    @pl.when(is_middle)
    def _():
        for slot in range(1, 4):
            relay(1, slot)
            side_relay(1, slot)

    def edge_relay(slot):
        @pl.when(middle == 0)
        def _():
            relay(1, slot)

    edge_relay(1)
    for piece in range(8):
        x_arrive(0, piece)

    @pl.loop(0, 4)
    def _(n):
        cols = pl.ds(pl.multiple_of(n * TILE, TILE), TILE)
        pre = jnp.dot(modded[...], w_ref[0, :, cols], preferred_element_type=F32)
        hid_ref[1, :, cols] = activation(pre, False).astype(BF16)
        pol = pre + jnp.dot(low_ref[...], b_ref[:, cols], preferred_element_type=F32)
        act, slope = activation(pol, True)
        hid_ref[0, :, cols] = act.astype(BF16)
        slope_ref[:, cols] = slope

    def y_core(j):
        src = ypart.at[j, 1 - core]
        return copy(src, crecv.at[j], c_send.at[j], c_recv.at[j], mate)

    def y_over(j):
        return copy(ysend.at[j], yrecv.at[j], y_send.at[j], y_recv.at[j], over)

    def v_copy(j, which):
        if which == 2:
            ref = vbuf.at[j, t_y]
        else:
            ref = vbuf.at[j, t]
        device = over if which == 1 else mate
        return copy(ref, ref, v_send.at[j, which], v_recv.at[j, which], device)

    def v_arrive(j, which):
        ref = vbuf.at[j, [t_core, t_y, t_far][which]]
        copy(ref, ref, v_send.at[j, which], v_recv.at[j, which], mate).wait_recv()

    def columns(j):
        return pl.ds(pl.multiple_of(place[j] * TILE, TILE), TILE)

    def stage_product(j):
        @pl.loop(0, 2)
        def _(p):
            part = contract_trailing(hid_ref[p], w_ref[1, pl.ds(place[j] * TILE, TILE), :])
            part = part.astype(BF16)
            for b in range(CAP):
                ypart[j, b % 2, b // 2, p] = part[b * BLK:(b + 1) * BLK, :]
        y_core(j).start()

    def stage_pair(j):
        y_core(j).wait_recv()
        ysend[j] = (ypart[j, core, 1 - y].astype(F32) + crecv[j, 1 - y].astype(F32)).astype(BF16)
        y_over(j).start()
        ysum[j] = ypart[j, core, y].astype(F32) + crecv[j, y].astype(F32)

    own = pl.ds(t * BLK, BLK)

    def stage_total(j):
        y_over(j).wait_recv()
        cols = columns(j)
        total = ysum[j] + yrecv[j].astype(F32)
        gate = mod_ref[t, 2:3, cols]
        residual = x_ref[own, cols].astype(F32) - t_ref[own, cols].astype(F32)
        mask = mask_ref[...]
        miss = residual + gate * total[0]
        miss_ref2 = residual + gate * total[1]
        slope = 2.0 * mask * miss
        miss_ref[:, cols] = slope
        vbuf[j, t] = (gate * slope).astype(BF16)
        v_copy(j, 0).start()
        v_copy(j, 1).start()
        err = jnp.concatenate([
            jnp.sum(mask * miss * miss, axis=(0, 1), keepdims=True),
            jnp.sum(mask * miss_ref2 * miss_ref2, axis=(0, 1), keepdims=True)], axis=0)
        return jnp.broadcast_to(err, (2, PAD))

    def stage_share(j):
        v_arrive(j, 1)
        v_copy(j, 2).start()

    def ready(j):
        x_arrive(1, 2 * j)
        x_arrive(1, 2 * j + 1)
        if j > 0:
            @pl.when(middle == 0)
            def _():
                side_relay(1, j)

    ready(0)
    stage_product(0)
    stage_pair(0)
    edge_relay(2)
    ready(1)
    stage_product(1)
    stage_pair(1)
    edge_relay(3)
    err = stage_total(0)
    ready(2)
    stage_product(2)
    stage_pair(2)
    err = err + stage_total(1)
    stage_share(0)
    ready(3)
    stage_product(3)
    stage_pair(3)
    err = err + stage_total(2)
    stage_share(1)
    err = err + stage_total(3)
    ebuf[t, 0:2, :] = err
    ebuf[t, 2:8, :] = jnp.zeros((6, PAD), F32)

    def e_copy(k):
        ref = ebuf.at[t]
        return copy(ref, ref, e_send.at[k], e_recv.at[k], peers[k])

    for k in range(3):
        e_copy(k).start()
    stage_share(2)
    stage_share(3)
    for k, peer in enumerate(peers):
        ref = ebuf.at[peer[1]]
        copy(ref, ref, e_send.at[k], e_recv.at[k], peer).wait_recv()
    gains = jnp.zeros((1, PAD), F32)
    loses = jnp.zeros((1, PAD), F32)
    for b in range(CAP):
        drop = ebuf[b, 0:1, :] - ebuf[b, 1:2, :]
        loser = flag_ref[b:b + 1, :]
        gains = gains + (1.0 - loser) * drop
        loses = loses + loser * drop
    inv_w, inv_l = 1.0 / (width * rows_w), 1.0 / (width * rows_l)
    outside = BETA * (gains * inv_w - loses * inv_l)
    loss = jnp.maximum(outside, 0.0) + jnp.log1p(jnp.exp(-jnp.abs(outside)))
    loss_ref[0] = loss[0, 0]
    weight = BETA * LOSS_SCALE / (1.0 + jnp.exp(-outside))
    loser = flag_ref[...]
    cf_ref[...] = weight * ((1.0 - loser) * inv_w - loser * inv_l)

    for j in range(4):
        v_arrive(j, 0)
        v_arrive(j, 2)

    @pl.loop(0, 4)
    def _(n):
        cols = pl.ds(pl.multiple_of(n * TILE, TILE), TILE)
        dh = jnp.zeros((CAP * BLK, TILE), F32)
        for j in range(4):
            dy = vbuf[j].reshape(CAP * BLK, TILE)
            dh = dh + jnp.dot(dy, w_ref[1, pl.ds(place[j] * TILE, TILE), cols],
                              preferred_element_type=F32)
        for b in range(CAP):
            block = slice(b * BLK, (b + 1) * BLK)
            dpre_ref[block, cols] = (
                dh[block] * (cf_ref[b:b + 1, 0:1] * slope_ref[block, cols])).astype(BF16)

    def dl_core():
        return copy(dlpart.at[1 - core], dlc, dc_send.at[4], dc_recv.at[4], mate)

    def dl_over():
        return copy(dlsend, dlrecv, dy_send.at[4], dy_recv.at[4], over)

    def dm_core(n):
        return copy(dmpart.at[n, 1 - core], dmc.at[n], dc_send.at[n], dc_recv.at[n], mate)

    def dm_over(n):
        return copy(dmsend.at[n], dmrecv.at[n], dy_send.at[n], dy_recv.at[n], over)

    def at_copy(k):
        return copy(gat.at[peers[k][1]], gatr.at[k], at_send.at[k], at_recv.at[k], peers[k])

    def rs_copy(which, k):
        to = (d + k) % 8
        part, land = ((gap, gapr), (gbp, gbr))[which]
        return copy(part.at[to], land.at[k], rs_send.at[which, k], rs_recv.at[which, k], (to, t))

    def ag_copy(which, k):
        to = (d + k) % 8
        ref = ga_ref.at[t, d] if which == 0 else gb_ref.at[d]
        return copy(ref, ref, ag_send.at[which, k], ag_recv.at[which, k], (to, t))

    def ag_arrive(which, k):
        source = (d + 8 - k) % 8
        ref = ga_ref.at[t, source] if which == 0 else gb_ref.at[source]
        copy(ref, ref, ag_send.at[which, k], ag_recv.at[which, k], (source, t)).wait_recv()

    dlowt = contract_trailing(b_ref[...], dpre_ref[...]).astype(BF16)
    ga = jnp.dot(dlowt, modded[...], preferred_element_type=F32).astype(BF16)
    for k in range(4):
        gat[k] = ga[k * 16:(k + 1) * 16, :]
    for k in range(3):
        at_copy(k).start()

    dlow = contract_trailing(dpre_ref[...], b_ref[...]).astype(BF16)
    for b in range(CAP):
        dlpart[b % 2, b // 2] = dlow[b * BLK:(b + 1) * BLK, :]
    dl_core().start()

    def dm_product(n):
        part = contract_trailing(
            dpre_ref[...], w_ref[0, n * TILE:(n + 1) * TILE, :]).astype(BF16)
        for b in range(CAP):
            dmpart[n, b % 2, b // 2] = part[b * BLK:(b + 1) * BLK, :]
        dm_core(n).start()

    def dm_pair(n):
        dm_core(n).wait_recv()
        dmsend[n] = (dmpart[n, core, 1 - y].astype(F32) + dmc[n, 1 - y].astype(F32)).astype(BF16)
        dm_over(n).start()
        dmsum[n] = dmpart[n, core, y].astype(F32) + dmc[n, y].astype(F32)

    dm_product(0)
    gb = jnp.dot(lowt_ref[...], dpre_ref[...], preferred_element_type=F32).astype(BF16)
    half_b = gb.shape[1] // 2
    for k in range(8):
        gbp[k] = gb[(k // 2) * 16:(k // 2 + 1) * 16, (k % 2) * half_b:(k % 2 + 1) * half_b]
    for k in range(1, 8):
        rs_copy(1, k).start()
    dm_pair(0)
    dl_core().wait_recv()
    dlsend[...] = (dlpart[core, 1 - y].astype(F32) + dlc[1 - y].astype(F32)).astype(BF16)
    dl_over().start()
    dlsum[...] = dlpart[core, y].astype(F32) + dlc[y].astype(F32)
    dm_product(1)
    total = gat[t].astype(F32)
    for k in range(3):
        at_copy(k).wait_recv()
        total = total + gatr[k].astype(F32)
    total = total.astype(BF16)
    wide = total.shape[1] // 8
    for k in range(8):
        gap[k] = total[:, k * wide:(k + 1) * wide]
    for k in range(1, 8):
        rs_copy(0, k).start()
    dm_pair(1)
    dm_product(2)
    dm_pair(2)
    dm_product(3)
    dm_pair(3)

    _, normed, inverse, _, scale, _ = norm(own, t)
    dl_over().wait_recv()
    dlow = (dlsum[...] + dlrecv[...].astype(F32)).astype(BF16)
    for n in range(4):
        dm_over(n).wait_recv()
    dm = jnp.concatenate([dmsum[n] + dmrecv[n].astype(F32) for n in range(4)], axis=1)
    dm = dm + jnp.dot(dlow, at_ref[...], preferred_element_type=F32)
    dn = dm * scale
    first = jnp.mean(dn, axis=-1, keepdims=True)
    second = jnp.mean(dn * normed, axis=-1, keepdims=True)
    out_grad = cf_ref[pl.ds(t, 1), 0:1] * miss_ref[...]
    grad_ref[t] = (out_grad + inverse * (dn - first - normed * second)).astype(BF16)

    def g_copy(which):
        ref = grad_ref.at[t_y] if which == 2 else grad_ref.at[t]
        return copy(ref, ref, g_send.at[which], g_recv.at[which], over if which == 1 else mate)

    def g_arrive(which):
        ref = grad_ref.at[[t_core, t_y, t_far][which]]
        copy(ref, ref, g_send.at[which], g_recv.at[which], mate).wait_recv()

    def g_store(k, block):
        return pltpu.make_async_copy(
            grad_ref.at[block], grad_out.at[pl.ds(block * BLK, BLK), :], local.at[7 + k])

    g_copy(1).start()
    g_copy(0).start()
    g_store(0, t).start()

    for which, (part, land) in ((1, (gbp, gbr)), (0, (gap, gapr))):
        total = part[d].astype(F32)
        for k in range(1, 8):
            rs_copy(which, k).wait_recv()
            total = total + land[k].astype(F32)
        if which == 1:
            gb_ref[d] = total.astype(BF16)
        else:
            ga_ref[t, d] = total.astype(BF16)
        for k in range(1, 8):
            ag_copy(which, k).start()

    g_arrive(1)
    g_copy(2).start()
    g_store(2, t_y).start()
    for k in range(1, 8):
        ag_arrive(0, k)

    def tg_copy(k):
        ref = ga_ref.at[t]
        return copy(ref, ref, tg_send.at[k], tg_recv.at[k], peers[k])

    for k in range(3):
        tg_copy(k).start()
    for k in range(1, 8):
        ag_arrive(1, k)
    for k in range(8):
        gb_out[(k // 2) * 16:(k // 2 + 1) * 16, (k % 2) * half_b:(k % 2 + 1) * half_b] = (
            gb_ref[k].astype(F32) * 0.125)
    g_arrive(0)
    g_store(1, t_core).start()
    g_arrive(2)
    g_store(3, t_far).start()
    for k, peer in enumerate(peers):
        ref = ga_ref.at[peer[1]]
        copy(ref, ref, tg_send.at[k], tg_recv.at[k], peer).wait_recv()
    for r in range(4):
        for k in range(8):
            gat_wide[r * 16:(r + 1) * 16, k * wide:(k + 1) * wide] = (
                ga_ref[r, k].astype(F32) * 0.125)
    gat_wide[rank:PAD, :] = jnp.zeros((PAD - rank, width), F32)
    ga_out[...] = gat_wide[...].T[:, 0:rank]
    for k, block in enumerate((t, t_core, t_y, t_far)):
        g_store(k, block).wait()

    for m in range(2):
        for piece in range(9):
            x_copy(m, piece).wait_send()
        for kind in range(3):
            z_copy(m, kind, 0).wait_send()

            @pl.when(is_middle)
            def _():
                for which in range(1, 5):
                    z_copy(m, kind, which).wait_send()
    for j in range(4):
        y_core(j).wait_send()
        y_over(j).wait_send()
        dm_core(j).wait_send()
        dm_over(j).wait_send()
        for which in range(3):
            v_copy(j, which).wait_send()
    dl_core().wait_send()
    dl_over().wait_send()
    for k in range(3):
        e_copy(k).wait_send()
        at_copy(k).wait_send()
        g_copy(k).wait_send()
        tg_copy(k).wait_send()
    for which in range(2):
        for k in range(1, 8):
            rs_copy(which, k).wait_send()
            ag_copy(which, k).wait_send()


def fused_device(
    tokens, targets, modulation, live_block_count, preferred_blocks, last_block_rows,
    up_projection_weight, down_weight_transposed, adapter_input_factor, adapter_output_factor,
):
    width = tokens.shape[1]
    rank = adapter_input_factor.shape[1]
    hidden = adapter_output_factor.shape[1]
    dma = pltpu.SemaphoreType.DMA
    vm = pltpu.VMEM
    rows = CAP * BLK
    smem = pl.BlockSpec(memory_space=pltpu.SMEM)
    anywhere = pl.BlockSpec(memory_space=pl.ANY)
    whole = pl.BlockSpec(memory_space=pltpu.VMEM)
    return pl.pallas_call(
        step_kernel,
        out_shape=(
            jax.ShapeDtypeStruct((1,), F32),
            jax.ShapeDtypeStruct((rows, width), BF16),
            jax.ShapeDtypeStruct((width, rank), F32),
            jax.ShapeDtypeStruct((rank, hidden), F32),
        ),
        in_specs=[smem] * 3 + [anywhere] * 7,
        out_specs=(smem, anywhere, whole, whole),
        scratch_shapes=[
            vm((rows, width), BF16),
            vm((rows, width), BF16),
            vm((2, 3, width), BF16),
            vm((width, rank), BF16),
            vm((PAD, hidden), BF16),
            vm((PAD, width), BF16),
            vm((CAP, 3, width), F32),
            vm((BLK, 1), F32),
            vm((8, PAD), F32),
            vm((CAP, BLK, width), BF16),
            vm((4, 8, 16, width // 8), BF16),
            vm((8, 16, hidden // 2), BF16),
            vm((PAD, width), F32),
            dma((11,)),
            vm((2, width, hidden), BF16),
            vm((rows, width), BF16),
            vm((rows, PAD), BF16),
            vm((PAD, rows), BF16),
            vm((rows, hidden), F32),
            vm((2, rows, hidden), BF16),
            vm((4, 2, 2, 2, BLK, TILE), BF16),
            vm((4, 2, 2, BLK, TILE), BF16),
            vm((4, 2, BLK, TILE), BF16),
            vm((4, 2, BLK, TILE), BF16),
            vm((4, 2, BLK, TILE), F32),
            vm((BLK, width), F32),
            vm((4, CAP, BLK, TILE), BF16),
            vm((CAP, 8, PAD), F32),
            vm((8, PAD), F32),
            vm((rows, hidden), BF16),
            vm((4, 2, 2, BLK, TILE), BF16),
            vm((4, 2, BLK, TILE), BF16),
            vm((4, BLK, TILE), BF16),
            vm((4, BLK, TILE), BF16),
            vm((4, BLK, TILE), F32),
            vm((2, 2, BLK, PAD), BF16),
            vm((2, BLK, PAD), BF16),
            vm((BLK, PAD), BF16),
            vm((BLK, PAD), BF16),
            vm((BLK, PAD), F32),
            vm((4, 16, width), BF16),
            vm((3, 16, width), BF16),
            vm((8, 16, width // 8), BF16),
            vm((8, 16, width // 8), BF16),
            vm((8, 16, hidden // 2), BF16),
            vm((8, 16, hidden // 2), BF16),
            dma((2, 3, 5)), dma((2, 3, 4)), dma((2, 9)), dma((2, 9)),
            dma((4,)), dma((4,)), dma((4,)), dma((4,)), dma((4, 3)), dma((4, 3)),
            dma((3,)), dma((3,)), dma((5,)), dma((5,)), dma((5,)), dma((5,)),
            dma((3,)), dma((3,)), dma((3,)), dma((3,)),
            dma((2, 8)), dma((2, 8)), dma((2, 8)), dma((2, 8)), dma((3,)), dma((3,)),
        ],
        compiler_params=pltpu.CompilerParams(
            collective_id=0, has_side_effects=True, vmem_limit_bytes=48 * 1024 * 1024),
    )(live_block_count, preferred_blocks, last_block_rows, tokens, targets, modulation,
      up_projection_weight, down_weight_transposed, adapter_input_factor, adapter_output_factor)


def fits_fused(mesh):
    return dict(mesh.shape) == {"dp": 8, "tensor": 4}


def solution(mesh):
    return jax.shard_map(
        fused_device if fits_fused(mesh) else per_device,
        mesh=mesh,
        in_specs=(
            P("dp", None),
            P("dp", None),
            P("dp", None, None),
            P("dp"),
            P("dp"),
            P("dp", None),
            P("dp", "tensor"),
            P("dp", "tensor"),
            P(),
            P(None, "tensor"),
        ),
        out_specs=(P("dp"), P("dp", None), P(), P(None, "tensor")),
        check_vma=False,
    )
```

profile of v0, /device:TPU:1, one launch (start us, length us, event | category | flops | bytes accessed | tf_op | source)
XLA Modules:
  0.0 151.6 jit_solution(10659258472473749527)
XLA Ops:
  0.6 0.0 copy-start.2
  2.0 0.7 copy.14.mod_hbm
  2.7 0.0 copy-start.5
  2.7 1.2 copy.15.a_hbm
  3.9 0.0 copy-done.2
  3.9 0.0 copy-done.5
  3.9 0.0 copy-start
  3.9 1.1 copy-done
  5.1 0.0 copy-start.1
  5.1 1.1 copy-done.1
  6.2 0.0 copy-start.3
  6.2 1.1 copy-done.3
  7.3 0.0 copy-start.4
  7.3 0.9 copy-done.4
  8.2 138.9 %shard_map.129 = (f32[1]{0:T(128)}, bf16[256,1536]{1,0:T(8,128)(2,1)S(1)}, f32[1536,64]{1,0:T(8,128)S(1)}, f32[64,1536]{1,0:T(8,128)S(1)}) custom-call(s32[1]{0:T(128)S(6)} %copy.20.live_ref, s32[1]{0:T(128)S(6)} %copy.21.wins_ref, s32[1,2]{1,0:T(1,128)S(1)} %copy-done.5, bf16[256,1536]{1,0:T(8,128)(2,1)S(1)} %copy-done, bf16[256,1536]{1,0:T(8,128)(2,1)S(1)} %copy-done.1, ...), custom_call_target="tpu_custom_call" | custom-call | tf_op jit(solution)/shard_map/pallas_call | solution.py:730
  147.1 1.0 copy.16
  148.8 0.9 copy.23
  149.7 0.7 copy.24
Async XLA Ops:
  0.6 3.3 %copy-start.2 = (bf16[192,1536]{1,0:T(8,128)(2,1)S(1)}, bf16[192,1536]{1,0:T(8,128)(2,1)}, u32[]{:S(2)}) copy-start(bf16[192,1536]{1,0:T(8,128)(2,1)} %up_ref.1) | copy-start | bytes 1769476
  2.7 1.2 copy-start.5
  3.9 1.1 copy-start
  5.1 1.1 copy-start.1
  6.2 1.1 copy-start.3
  7.3 0.9 copy-start.4
where the time goes:
time: 152 us
  Pallas kernels  139 us (91%)
  local copies, waits for them, and re-layouts  8.77 us (6%)
  between operations  3.87 us (3%)
    pallas_call x1, Pallas kernels, fused_device(): pl.pallas_call(step_kernel, out_shape=(jax.ShapeDtypeStruct((1,), F32), j...  139 us
    unnamed x16, local copies, waits for them, and re-layouts  7.78 us

commit v1 on v0

--- a/solution.py
+++ b/solution.py
@@ -186,8 +186,8 @@
 def step_kernel(
     live_ref, wins_ref, tail_ref, x_hbm, t_hbm, mod_hbm, up_ref, dn_ref, a_hbm, b_hbm,
     loss_ref, grad_out, ga_out, gb_out,
-    x_ref, t_ref, mod_in, a_in, b_ref, at_ref, mod_ref, mask_ref, flag_ref,
-    grad_ref, ga_ref, gb_ref, gat_wide, local,
+    x_ref, t_ref, mod_in, b_ref, at_ref, mod_ref, mask_ref, flag_ref,
+    grad_ref, ga_ref, gb_ref, local,
     w_ref, modded, low_ref, lowt_ref, slope_ref, hid_ref,
     ypart, crecv, ysend, yrecv, ysum, miss_ref, vbuf, ebuf, cf_ref,
     dpre_ref, dmpart, dmc, dmsend, dmrecv, dmsum,
@@ -231,7 +231,8 @@
     loads = [
         pltpu.make_async_copy(src, dst, local.at[k]) for k, (src, dst) in enumerate((
             (up_ref, w_ref.at[0, here, :]), (dn_ref, w_ref.at[1, here, :]),
-            (x_hbm, x_ref), (mod_hbm, mod_in), (a_hbm, a_in),
+            (x_hbm, x_ref), (mod_hbm, mod_in),
+            (a_hbm, at_ref.at[pl.ds(0, a_hbm.shape[0]), :]),
             (b_hbm, b_ref.at[pl.ds(0, b_hbm.shape[0]), :]), (t_hbm, t_ref)))]
     for load in loads:
         load.start()
@@ -275,9 +276,12 @@
         copy(ref, ref, x_send.at[m, piece], x_recv.at[m, piece], across).wait_recv()
 
     def begin_inner(m):
+        for part in range(2):
+            z_copy(m, part, 0).start()
+
+    def begin_x(m):
         x_copy(m, 8).start()
         for part in range(2):
-            z_copy(m, part, 0).start()
             x_copy(m, part).start()
 
     def begin_edge(m):
@@ -294,15 +298,18 @@
         def _():
             z_copy(m, 2, 1).start()
 
+    def relay_part(m, slot, part):
+        z_arrive(m, part, slot)
+
+        @pl.when(is_middle)
+        def _():
+            z_copy(m, part, slot + 1).start()
+
+        x_copy(m, slot * 2 + part).start()
+
     def relay(m, slot):
         for part in range(2):
-            z_arrive(m, part, slot)
-
-            @pl.when(is_middle)
-            def _():
-                z_copy(m, part, slot + 1).start()
-
-            x_copy(m, slot * 2 + part).start()
+            relay_part(m, slot, part)
 
     def side_relay(m, slot):
         z_arrive(m, 2, slot)
@@ -313,6 +320,7 @@
 
     begin_edge(0)
     begin_inner(0)
+    begin_x(0)
 
     count, wins = live_ref[0], wins_ref[0]
     tail_w, tail_l = tail_ref[0, 0], tail_ref[0, 1]
@@ -329,14 +337,13 @@
     rows_l = jnp.broadcast_to(((count - wins - 1) * BLK + tail_l).astype(F32), (1, PAD))
     for load in loads[2:]:
         load.wait()
-    rank = a_in.shape[1]
+    rank = a_hbm.shape[0]
     b_ref[rank:PAD, :] = jnp.zeros((PAD - rank, b_ref.shape[1]), BF16)
-    a_wide = jnp.concatenate(
-        [a_in[...].astype(F32), jnp.zeros((width, PAD - rank), F32)], axis=1)
-    at_ref[...] = a_wide.T.astype(BF16)
+    at_ref[rank:PAD, :] = jnp.zeros((PAD - rank, width), BF16)
     for b in range(CAP):
         loser = flag_ref[b:b + 1, 0:1]
-        mod_ref[b] = (1.0 - loser) * mod_in[0].astype(F32) + loser * mod_in[1].astype(F32)
+        mod_ref[b] = ((1.0 - loser) * mod_in[:, 0, :].astype(F32)
+                      + loser * mod_in[:, 1, :].astype(F32))
 
     def norm(block, b):
         wide = x_ref[block, :].astype(F32)
@@ -356,12 +363,22 @@
 
     side_begin(0)
     relay(0, 1)
-    begin_inner(1)
+
+    @pl.when(middle == 0)
+    def _():
+        begin_inner(1)
+
+    begin_x(1)
     side_relay(0, 1)
     relay(0, 2)
     side_relay(0, 2)
     relay(0, 3)
     side_relay(0, 3)
+
+    @pl.when(is_middle)
+    def _():
+        begin_inner(1)
+
     begin_edge(1)
     side_begin(1)
 
@@ -371,10 +388,11 @@
             relay(1, slot)
             side_relay(1, slot)
 
-    def edge_relay(slot):
+    def edge_relay(slot, parts=(0, 1)):
         @pl.when(middle == 0)
         def _():
-            relay(1, slot)
+            for part in parts:
+                relay_part(1, slot, part)
 
     edge_relay(1)
     for piece in range(8):
@@ -467,18 +485,19 @@
     ready(1)
     stage_product(1)
     stage_pair(1)
-    edge_relay(3)
     err = stage_total(0)
+    edge_relay(3, (0,))
     ready(2)
     stage_product(2)
     stage_pair(2)
+    edge_relay(3, (1,))
     err = err + stage_total(1)
     stage_share(0)
+    err = err + stage_total(2)
+    stage_share(1)
     ready(3)
     stage_product(3)
     stage_pair(3)
-    err = err + stage_total(2)
-    stage_share(1)
     err = err + stage_total(3)
     ebuf[t, 0:2, :] = err
     ebuf[t, 2:8, :] = jnp.zeros((6, PAD), F32)
@@ -677,10 +696,8 @@
         copy(ref, ref, tg_send.at[k], tg_recv.at[k], peer).wait_recv()
     for r in range(4):
         for k in range(8):
-            gat_wide[r * 16:(r + 1) * 16, k * wide:(k + 1) * wide] = (
+            ga_out[r * 16:(r + 1) * 16, k * wide:(k + 1) * wide] = (
                 ga_ref[r, k].astype(F32) * 0.125)
-    gat_wide[rank:PAD, :] = jnp.zeros((PAD - rank, width), F32)
-    ga_out[...] = gat_wide[...].T[:, 0:rank]
     for k, block in enumerate((t, t_core, t_y, t_far)):
         g_store(k, block).wait()
 
@@ -727,12 +744,12 @@
     smem = pl.BlockSpec(memory_space=pltpu.SMEM)
     anywhere = pl.BlockSpec(memory_space=pl.ANY)
     whole = pl.BlockSpec(memory_space=pltpu.VMEM)
-    return pl.pallas_call(
+    losses, grad, grad_a, grad_b = pl.pallas_call(
         step_kernel,
         out_shape=(
             jax.ShapeDtypeStruct((1,), F32),
             jax.ShapeDtypeStruct((rows, width), BF16),
-            jax.ShapeDtypeStruct((width, rank), F32),
+            jax.ShapeDtypeStruct((rank, width), F32),
             jax.ShapeDtypeStruct((rank, hidden), F32),
         ),
         in_specs=[smem] * 3 + [anywhere] * 7,
@@ -740,8 +757,7 @@
         scratch_shapes=[
             vm((rows, width), BF16),
             vm((rows, width), BF16),
-            vm((2, 3, width), BF16),
-            vm((width, rank), BF16),
+            vm((3, 2, width), BF16),
             vm((PAD, hidden), BF16),
             vm((PAD, width), BF16),
             vm((CAP, 3, width), F32),
@@ -750,7 +766,6 @@
             vm((CAP, BLK, width), BF16),
             vm((4, 8, 16, width // 8), BF16),
             vm((8, 16, hidden // 2), BF16),
-            vm((PAD, width), F32),
             dma((11,)),
             vm((2, width, hidden), BF16),
             vm((rows, width), BF16),
@@ -791,9 +806,11 @@
             dma((2, 8)), dma((2, 8)), dma((2, 8)), dma((2, 8)), dma((3,)), dma((3,)),
         ],
         compiler_params=pltpu.CompilerParams(
-            collective_id=0, has_side_effects=True, vmem_limit_bytes=48 * 1024 * 1024),
-    )(live_block_count, preferred_blocks, last_block_rows, tokens, targets, modulation,
-      up_projection_weight, down_weight_transposed, adapter_input_factor, adapter_output_factor)
+            collective_id=0, has_side_effects=True, vmem_limit_bytes=60 * 1024 * 1024),
+    )(live_block_count, preferred_blocks, last_block_rows, tokens, targets,
+      modulation.transpose(1, 0, 2), up_projection_weight, down_weight_transposed,
+      adapter_input_factor.T, adapter_output_factor)
+    return losses, grad, grad_a.T, grad_b
 
 
 def fits_fused(mesh):

time: 152 us -> 147 us (0.967)
  local copies, waits for them, and re-layouts: 8.77 us -> 4 us
    unnamed x16 -> x7, local copies, waits for them, and re-layouts: 7.78 us -> 4 us
where the time goes in v1:
time: 147 us
  Pallas kernels  139 us (95%)
  local copies, waits for them, and re-layouts  4 us (3%)
  between operations  3.7 us (3%)
    pallas_call x1, Pallas kernels, fused_device(): pl.pallas_call(step_kernel, out_shape=(jax.ShapeDtypeStruct((1,), F32), j...  139 us
    unnamed x7, local copies, waits for them, and re-layouts  4 us

profile of v1, /device:TPU:1, one launch (start us, length us, event | category | flops | bytes accessed | tf_op | source)
XLA Modules:
  0.0 147.1 jit_solution(17885555737312772447)
XLA Ops:
  1.9 139.4 %shard_map.129 = (f32[1]{0:T(128)}, bf16[256,1536]{1,0:T(8,128)(2,1)}, f32[64,1536]{1,0:T(8,128)}, f32[64,1536]{1,0:T(8,128)}) custom-call(s32[1]{0:T(128)S(6)} %copy.18.live_ref, s32[1]{0:T(128)S(6)} %copy.19.wins_ref, s32[1,2]{1,0:T(1,128)} %tail_ref.1, bf16[256,1536]{1,0:T(8,128)(2,1)} %x_hbm.1, bf16[256,1536]{1,0:T(8,128)(2,1)} %t_hbm.1, ...), custom_call_target="tpu_custom_call" | custom-call | tf_op jit(solution)/shard_map/pallas_call | solution.py:747
  141.9 0.0 copy-start.1
  141.9 2.1 %copy.21 = bf16[256,1536]{1,0:T(8,128)(2,1)} copy(bf16[256,1536]{1,0:T(8,128)(2,1)} %get-tuple-element.17) | data formatting | bytes 1572864
  144.1 0.0 copy-done.1
  144.1 0.0 copy-start
  144.1 0.7 copy.22
  144.8 0.4 copy-done
  145.2 0.7 copy.23
Async XLA Ops:
  141.9 2.1 %copy-start.1 = (f32[64,1536]{1,0:T(8,128)S(1)}, f32[64,1536]{1,0:T(8,128)}, u32[]{:S(2)}) copy-start(f32[64,1536]{1,0:T(8,128)} %get-tuple-element.10) | copy-start | bytes 1179652
  144.1 1.1 copy-start

commit v2 on v1

--- a/solution.py
+++ b/solution.py
@@ -284,41 +284,56 @@
         for part in range(2):
             x_copy(m, part).start()
 
-    def begin_edge(m):
+    def outward(i):
+        return z_copy(i // 9, i % 3, (1, 3, 4)[i % 9 // 3])
+
+    def push(*items):
         @pl.when(is_middle)
         def _():
-            for part in range(2):
-                z_copy(m, part, 1).start()
+            for i in items:
+                m, kind, slot = i // 9, i % 3, (0, 2, 3)[i % 9 // 3]
+                if slot > 0:
+                    z_arrive(m, kind, slot)
+                    if kind < 2:
+                        x_copy(m, slot * 2 + kind).start()
+                if i > 1:
+                    outward(i - 2).wait_send()
+                outward(i).start()
+
+    def edge_relay(m, slot, parts=(0, 1)):
+        @pl.when(middle == 0)
+        def _():
+            for part in parts:
+                z_arrive(m, part, slot)
+                x_copy(m, slot * 2 + part).start()
+
+    def edge_side(m, slot):
+        @pl.when(middle == 0)
+        def _():
+            z_arrive(m, 2, slot)
+
+    def first_relay(m):
+        for part in range(2):
+            z_arrive(m, part, 1)
+
+            @pl.when(is_middle)
+            def _():
+                z_copy(m, part, 2).start()
+
+            x_copy(m, 2 + part).start()
+
+    def first_side(m):
+        z_arrive(m, 2, 1)
+
+        @pl.when(is_middle)
+        def _():
+            z_copy(m, 2, 2).start()
 
     def side_begin(m):
         x_arrive(m, 8)
         z_copy(m, 2, 0).start()
 
-        @pl.when(is_middle)
-        def _():
-            z_copy(m, 2, 1).start()
-
-    def relay_part(m, slot, part):
-        z_arrive(m, part, slot)
-
-        @pl.when(is_middle)
-        def _():
-            z_copy(m, part, slot + 1).start()
-
-        x_copy(m, slot * 2 + part).start()
-
-    def relay(m, slot):
-        for part in range(2):
-            relay_part(m, slot, part)
-
-    def side_relay(m, slot):
-        z_arrive(m, 2, slot)
-
-        @pl.when(is_middle)
-        def _():
-            z_copy(m, 2, slot + 1).start()
-
-    begin_edge(0)
+    push(0, 1)
     begin_inner(0)
     begin_x(0)
 
@@ -362,39 +377,37 @@
     lowt_ref[...] = contract_trailing(at_ref[...], modded[...]).astype(BF16)
 
     side_begin(0)
-    relay(0, 1)
+    push(2)
+    first_relay(0)
 
     @pl.when(middle == 0)
     def _():
         begin_inner(1)
 
+    first_side(0)
+    edge_relay(0, 2)
+    push(3, 4)
     begin_x(1)
-    side_relay(0, 1)
-    relay(0, 2)
-    side_relay(0, 2)
-    relay(0, 3)
-    side_relay(0, 3)
+    edge_side(0, 2)
+    push(5)
 
     @pl.when(is_middle)
     def _():
         begin_inner(1)
 
-    begin_edge(1)
+    edge_relay(0, 3)
+    push(6, 7)
+    edge_side(0, 3)
+    push(8, 9, 10)
     side_begin(1)
+    push(11)
+    first_relay(1)
 
     @pl.when(is_middle)
     def _():
-        for slot in range(1, 4):
-            relay(1, slot)
-            side_relay(1, slot)
-
-    def edge_relay(slot, parts=(0, 1)):
-        @pl.when(middle == 0)
-        def _():
-            for part in parts:
-                relay_part(1, slot, part)
-
-    edge_relay(1)
+        z_arrive(1, 2, 1)
+        z_copy(1, 2, 2).start()
+
     for piece in range(8):
         x_arrive(0, piece)
 
@@ -474,23 +487,26 @@
         x_arrive(1, 2 * j)
         x_arrive(1, 2 * j + 1)
         if j > 0:
-            @pl.when(middle == 0)
-            def _():
-                side_relay(1, j)
-
+            edge_side(1, j)
+
+    push(12)
     ready(0)
     stage_product(0)
+    push(13)
     stage_pair(0)
-    edge_relay(2)
+    push(14)
+    edge_relay(1, 2)
     ready(1)
     stage_product(1)
     stage_pair(1)
+    push(15, 16)
     err = stage_total(0)
-    edge_relay(3, (0,))
+    edge_relay(1, 3, (0,))
     ready(2)
     stage_product(2)
+    push(17)
     stage_pair(2)
-    edge_relay(3, (1,))
+    edge_relay(1, 3, (1,))
     err = err + stage_total(1)
     stage_share(0)
     err = err + stage_total(2)
@@ -709,8 +725,12 @@
 
             @pl.when(is_middle)
             def _():
-                for which in range(1, 5):
-                    z_copy(m, kind, which).wait_send()
+                z_copy(m, kind, 2).wait_send()
+
+    @pl.when(is_middle)
+    def _():
+        outward(16).wait_send()
+        outward(17).wait_send()
     for j in range(4):
         y_core(j).wait_send()
         y_over(j).wait_send()

time: 147 us -> 149 us (1.014)
  Pallas kernels: 139 us -> 141 us
where the time goes in v2:
time: 149 us; the launch traced here: 148 us
  Pallas kernels  141 us (95%)
  local copies, waits for them, and re-layouts  4 us (3%)
  between operations  3.7 us (2%)
    pallas_call x1, Pallas kernels, fused_device(): pl.pallas_call(step_kernel, out_shape=(jax.ShapeDtypeStruct((1,), F32), j...  141 us
    unnamed x7, local copies, waits for them, and re-layouts  4 us

profile of v2, /device:TPU:1, one launch (start us, length us, event | category | flops | bytes accessed | tf_op | source)
XLA Modules:
  0.0 148.5 jit_solution(2013432163680007911)
XLA Ops:
  1.9 140.8 %shard_map.129 = (f32[1]{0:T(128)}, bf16[256,1536]{1,0:T(8,128)(2,1)}, f32[64,1536]{1,0:T(8,128)}, f32[64,1536]{1,0:T(8,128)}) custom-call(s32[1]{0:T(128)S(6)} %copy.18.live_ref, s32[1]{0:T(128)S(6)} %copy.19.wins_ref, s32[1,2]{1,0:T(1,128)} %tail_ref.1, bf16[256,1536]{1,0:T(8,128)(2,1)} %x_hbm.1, bf16[256,1536]{1,0:T(8,128)(2,1)} %t_hbm.1, ...), custom_call_target="tpu_custom_call" | custom-call | tf_op jit(solution)/shard_map/pallas_call | solution.py:767
  143.3 0.0 copy-start.1
  143.3 2.1 %copy.21 = bf16[256,1536]{1,0:T(8,128)(2,1)} copy(bf16[256,1536]{1,0:T(8,128)(2,1)} %get-tuple-element.17) | data formatting | bytes 1572864
  145.4 0.0 copy-done.1
  145.4 0.0 copy-start
  145.4 0.7 copy.22
  146.2 0.4 copy-done
  146.6 0.7 copy.23
Async XLA Ops:
  143.3 2.1 %copy-start.1 = (f32[64,1536]{1,0:T(8,128)S(1)}, f32[64,1536]{1,0:T(8,128)}, u32[]{:S(2)}) copy-start(f32[64,1536]{1,0:T(8,128)} %get-tuple-element.10) | copy-start | bytes 1179652
  145.4 1.1 copy-start

commit v3 on v1

--- a/solution.py
+++ b/solution.py
@@ -187,7 +187,7 @@
     live_ref, wins_ref, tail_ref, x_hbm, t_hbm, mod_hbm, up_ref, dn_ref, a_hbm, b_hbm,
     loss_ref, grad_out, ga_out, gb_out,
     x_ref, t_ref, mod_in, b_ref, at_ref, mod_ref, mask_ref, flag_ref,
-    grad_ref, ga_ref, gb_ref, local,
+    grad_ref, ga_ref, gb_ref, ga_rows, local,
     w_ref, modded, low_ref, lowt_ref, slope_ref, hid_ref,
     ypart, crecv, ysend, yrecv, ysum, miss_ref, vbuf, ebuf, cf_ref,
     dpre_ref, dmpart, dmc, dmsend, dmrecv, dmsum,
@@ -236,8 +236,6 @@
             (b_hbm, b_ref.at[pl.ds(0, b_hbm.shape[0]), :]), (t_hbm, t_ref)))]
     for load in loads:
         load.start()
-    loads[0].wait()
-    loads[1].wait()
     pl.semaphore_wait(barrier, 10)
 
     def copy(src, dst, send, recv, device):
@@ -261,7 +259,11 @@
         target = [1 + middle, 1, 3, 2, 3][which]
         device = inner if which in (0, 2) else edge
         ref = rows(m, kind, slot)
-        return copy(ref, ref, z_send.at[m, kind, which], z_recv.at[m, kind, target], device)
+        src = ref
+        if slot == 0 and kind < 2:
+            start = (0, half)[kind]
+            src = (up_ref, dn_ref)[m].at[pl.ds(start, (half, shard - half)[kind]), :]
+        return copy(src, ref, z_send.at[m, kind, which], z_recv.at[m, kind, target], device)
 
     def z_arrive(m, kind, slot):
         ref = rows(m, kind, slot)
@@ -269,7 +271,11 @@
 
     def x_copy(m, piece):
         ref = x_rows(m, piece, x)
-        return copy(ref, ref, x_send.at[m, piece], x_recv.at[m, piece], across)
+        src = ref
+        if piece in (0, 1, 8):
+            start, size = {0: (0, half), 1: (half, half), 8: (main, SIDE)}[piece]
+            src = (up_ref, dn_ref)[m].at[pl.ds(start, size), :]
+        return copy(src, ref, x_send.at[m, piece], x_recv.at[m, piece], across)
 
     def x_arrive(m, piece):
         ref = x_rows(m, piece, 1 - x)
@@ -335,7 +341,7 @@
     width = x_ref.shape[1]
     rows_w = jnp.broadcast_to(((wins - 1) * BLK + tail_w).astype(F32), (1, PAD))
     rows_l = jnp.broadcast_to(((count - wins - 1) * BLK + tail_l).astype(F32), (1, PAD))
-    for load in loads[2:]:
+    for load in loads:
         load.wait()
     rank = a_hbm.shape[0]
     b_ref[rank:PAD, :] = jnp.zeros((PAD - rank, b_ref.shape[1]), BF16)
@@ -416,15 +422,12 @@
         return copy(ysend.at[j], yrecv.at[j], y_send.at[j], y_recv.at[j], over)
 
     def v_copy(j, which):
-        if which == 2:
-            ref = vbuf.at[j, t_y]
-        else:
-            ref = vbuf.at[j, t]
+        ref = vbuf.at[t_y if which == 2 else t, :, columns(j)]
         device = over if which == 1 else mate
         return copy(ref, ref, v_send.at[j, which], v_recv.at[j, which], device)
 
     def v_arrive(j, which):
-        ref = vbuf.at[j, [t_core, t_y, t_far][which]]
+        ref = vbuf.at[[t_core, t_y, t_far][which], :, columns(j)]
         copy(ref, ref, v_send.at[j, which], v_recv.at[j, which], mate).wait_recv()
 
     def columns(j):
@@ -458,7 +461,7 @@
         miss_ref2 = residual + gate * total[1]
         slope = 2.0 * mask * miss
         miss_ref[:, cols] = slope
-        vbuf[j, t] = (gate * slope).astype(BF16)
+        vbuf[t, :, cols] = (gate * slope).astype(BF16)
         v_copy(j, 0).start()
         v_copy(j, 1).start()
         err = jnp.concatenate([
@@ -535,11 +538,8 @@
     @pl.loop(0, 4)
     def _(n):
         cols = pl.ds(pl.multiple_of(n * TILE, TILE), TILE)
-        dh = jnp.zeros((CAP * BLK, TILE), F32)
-        for j in range(4):
-            dy = vbuf[j].reshape(CAP * BLK, TILE)
-            dh = dh + jnp.dot(dy, w_ref[1, pl.ds(place[j] * TILE, TILE), cols],
-                              preferred_element_type=F32)
+        dy = vbuf[...].reshape(CAP * BLK, vbuf.shape[2])
+        dh = jnp.dot(dy, w_ref[1, :, cols], preferred_element_type=F32)
         for b in range(CAP):
             block = slice(b * BLK, (b + 1) * BLK)
             dpre_ref[block, cols] = (
@@ -629,6 +629,18 @@
     dm_product(3)
     dm_pair(3)
 
+    for which, (part, land) in ((0, (gap, gapr)), (1, (gbp, gbr))):
+        total = part[d].astype(F32)
+        for k in range(1, 8):
+            rs_copy(which, k).wait_recv()
+            total = total + land[k].astype(F32)
+        if which == 1:
+            gb_ref[d] = total.astype(BF16)
+        else:
+            ga_ref[t, d] = total.astype(BF16)
+        for k in range(1, 8):
+            ag_copy(which, k).start()
+
     _, normed, inverse, _, scale, _ = norm(own, t)
     dl_over().wait_recv()
     dlow = (dlsum[...] + dlrecv[...].astype(F32)).astype(BF16)
@@ -640,6 +652,20 @@
     first = jnp.mean(dn, axis=-1, keepdims=True)
     second = jnp.mean(dn * normed, axis=-1, keepdims=True)
     out_grad = cf_ref[pl.ds(t, 1), 0:1] * miss_ref[...]
+    for k in range(1, 8):
+        ag_arrive(0, k)
+    for k in range(8):
+        ga_rows[t, :, k * wide:(k + 1) * wide] = ga_ref[t, k]
+
+    def tg_copy(which):
+        ref = ga_rows.at[t_y if which == 2 else t]
+        return copy(ref, ref, tg_send.at[which], tg_recv.at[which],
+                    over if which == 1 else mate)
+
+    def tg_arrive(which):
+        ref = ga_rows.at[[t_core, t_y, t_far][which]]
+        copy(ref, ref, tg_send.at[which], tg_recv.at[which], mate).wait_recv()
+
     grad_ref[t] = (out_grad + inverse * (dn - first - normed * second)).astype(BF16)
 
     def g_copy(which):
@@ -656,48 +682,27 @@
 
     g_copy(1).start()
     g_copy(0).start()
+    tg_copy(1).start()
+    tg_copy(0).start()
     g_store(0, t).start()
-
-    for which, (part, land) in ((1, (gbp, gbr)), (0, (gap, gapr))):
-        total = part[d].astype(F32)
-        for k in range(1, 8):
-            rs_copy(which, k).wait_recv()
-            total = total + land[k].astype(F32)
-        if which == 1:
-            gb_ref[d] = total.astype(BF16)
-        else:
-            ga_ref[t, d] = total.astype(BF16)
-        for k in range(1, 8):
-            ag_copy(which, k).start()
 
     g_arrive(1)
     g_copy(2).start()
     g_store(2, t_y).start()
-    for k in range(1, 8):
-        ag_arrive(0, k)
-
-    def tg_copy(k):
-        ref = ga_ref.at[t]
-        return copy(ref, ref, tg_send.at[k], tg_recv.at[k], peers[k])
-
-    for k in range(3):
-        tg_copy(k).start()
+    tg_arrive(1)
+    tg_copy(2).start()
     for k in range(1, 8):
         ag_arrive(1, k)
     for k in range(8):
         gb_out[(k // 2) * 16:(k // 2 + 1) * 16, (k % 2) * half_b:(k % 2 + 1) * half_b] = (
-            gb_ref[k].astype(F32) * 0.125)
+            gb_ref[k])
     g_arrive(0)
     g_store(1, t_core).start()
     g_arrive(2)
     g_store(3, t_far).start()
-    for k, peer in enumerate(peers):
-        ref = ga_ref.at[peer[1]]
-        copy(ref, ref, tg_send.at[k], tg_recv.at[k], peer).wait_recv()
-    for r in range(4):
-        for k in range(8):
-            ga_out[r * 16:(r + 1) * 16, k * wide:(k + 1) * wide] = (
-                ga_ref[r, k].astype(F32) * 0.125)
+    tg_arrive(0)
+    tg_arrive(2)
+    ga_out[...] = ga_rows[...].reshape(ga_out.shape)
     for k, block in enumerate((t, t_core, t_y, t_far)):
         g_store(k, block).wait()
 
@@ -749,8 +754,8 @@
         out_shape=(
             jax.ShapeDtypeStruct((1,), F32),
             jax.ShapeDtypeStruct((rows, width), BF16),
-            jax.ShapeDtypeStruct((rank, width), F32),
-            jax.ShapeDtypeStruct((rank, hidden), F32),
+            jax.ShapeDtypeStruct((rank, width), BF16),
+            jax.ShapeDtypeStruct((rank, hidden), BF16),
         ),
         in_specs=[smem] * 3 + [anywhere] * 7,
         out_specs=(smem, anywhere, whole, whole),
@@ -766,6 +771,7 @@
             vm((CAP, BLK, width), BF16),
             vm((4, 8, 16, width // 8), BF16),
             vm((8, 16, hidden // 2), BF16),
+            vm((4, 16, width), BF16),
             dma((11,)),
             vm((2, width, hidden), BF16),
             vm((rows, width), BF16),
@@ -779,7 +785,7 @@
             vm((4, 2, BLK, TILE), BF16),
             vm((4, 2, BLK, TILE), F32),
             vm((BLK, width), F32),
-            vm((4, CAP, BLK, TILE), BF16),
+            vm((CAP, BLK, width), BF16),
             vm((CAP, 8, PAD), F32),
             vm((8, PAD), F32),
             vm((rows, hidden), BF16),
@@ -810,7 +816,8 @@
     )(live_block_count, preferred_blocks, last_block_rows, tokens, targets,
       modulation.transpose(1, 0, 2), up_projection_weight, down_weight_transposed,
       adapter_input_factor.T, adapter_output_factor)
-    return losses, grad, grad_a.T, grad_b
+    n_dp = lax.axis_size("dp")
+    return losses, grad, grad_a.T.astype(F32) / n_dp, grad_b.astype(F32) / n_dp
 
 
 def fits_fused(mesh):

time: 147 us -> 146 us (level)
  local copies, waits for them, and re-layouts: 4 us -> 0.89 us
  other arithmetic: 0 us -> 2.05 us
    unnamed x7 -> x3, local copies, waits for them, and re-layouts: 4 us -> 0.89 us
    div x0 -> x1, other arithmetic: none -> 2.05 us  [fused_device(): grad_b.astype(F32) / n_dp]
where the time goes in v3:
time: 146 us
  Pallas kernels  139 us (95%)
  between operations  3.72 us (3%)
  other arithmetic  2.05 us (1%)
    pallas_call x1, Pallas kernels, fused_device(): pl.pallas_call(step_kernel, out_shape=(jax.ShapeDtypeStruct((1,), F32), j...  139 us

profile of v3, /device:TPU:1, one launch (start us, length us, event | category | flops | bytes accessed | tf_op | source)
XLA Modules:
  0.0 145.6 jit_solution(5314547536288630851)
XLA Ops:
  1.9 138.9 %shard_map.129 = (f32[1]{0:T(128)}, bf16[256,1536]{1,0:T(8,128)(2,1)}, bf16[64,1536]{1,0:T(8,128)(2,1)}, bf16[64,1536]{1,0:T(8,128)(2,1)}) custom-call(s32[1]{0:T(128)S(6)} %copy.16.live_ref, s32[1]{0:T(128)S(6)} %copy.17.wins_ref, s32[1,2]{1,0:T(1,128)} %tail_ref.1, bf16[256,1536]{1,0:T(8,128)(2,1)} %x_hbm.1, bf16[256,1536]{1,0:T(8,128)(2,1)} %t_hbm.1, ...), custom_call_target="tpu_custom_call" | custom-call | tf_op jit(solution)/shard_map/pallas_call | solution.py:752
  140.9 0.0 copy-start
  140.9 2.0 %convert_multiply_fusion = (f32[64,1536]{1,0:T(8,128)}, f32[1536,64]{0,1:T(8,128)}) fusion(bf16[64,1536]{1,0:T(8,128)(2,1)} %get-tuple-element.11, bf16[64,1536]{1,0:T(8,128)(2,1)} %get-tuple-element.10), kind=kLoop, calls=%fused_computation | loop fusion | flops 393216 | bytes 1179648 | tf_op jit(solution)/shard_map/div | solution.py:820
  143.6 0.0 copy-done
  143.6 0.9 copy.19
Async XLA Ops:
  140.9 2.7 %copy-start = (bf16[256,1536]{1,0:T(8,128)(2,1)S(1)}, bf16[256,1536]{1,0:T(8,128)(2,1)}, u32[]{:S(2)}) copy-start(bf16[256,1536]{1,0:T(8,128)(2,1)} %get-tuple-element.19) | copy-start | bytes 2359300

commit v4 on v3

--- a/solution.py
+++ b/solution.py
@@ -169,6 +169,7 @@
 SIDE = 32
 TILE = 384
 PAD = 128
+STRIP = 16
 GELU_ROOT = 0.7978845608028654
 GELU_CUBE = 0.044715
 
@@ -187,7 +188,7 @@
     live_ref, wins_ref, tail_ref, x_hbm, t_hbm, mod_hbm, up_ref, dn_ref, a_hbm, b_hbm,
     loss_ref, grad_out, ga_out, gb_out,
     x_ref, t_ref, mod_in, b_ref, at_ref, mod_ref, mask_ref, flag_ref,
-    grad_ref, ga_ref, gb_ref, ga_rows, local,
+    grad_ref, ga_ref, gb_ref, ga_rows, pre_ref, back_ref, local,
     w_ref, modded, low_ref, lowt_ref, slope_ref, hid_ref,
     ypart, crecv, ysend, yrecv, ysum, miss_ref, vbuf, ebuf, cf_ref,
     dpre_ref, dmpart, dmc, dmsend, dmrecv, dmsum,
@@ -358,10 +359,10 @@
         vectors = mod_ref[b]
         return wide, center * inverse, inverse, vectors[0:1], 1.0 + vectors[1:2], vectors[2:3]
 
-    @pl.loop(0, CAP)
-    def _(b):
-        block = pl.ds(b * BLK, BLK)
-        _, normed, _, shift, scale, _ = norm(block, b)
+    @pl.loop(0, CAP * BLK // STRIP)
+    def _(i):
+        block = pl.ds(pl.multiple_of(i * STRIP, STRIP), STRIP)
+        _, normed, _, shift, scale, _ = norm(block, i // (BLK // STRIP))
         modded[block, :] = (normed * scale + shift).astype(BF16)
 
     low_ref[...] = contract_trailing(modded[...], at_ref[...]).astype(BF16)
@@ -408,11 +409,16 @@
     def _(n):
         cols = pl.ds(pl.multiple_of(n * TILE, TILE), TILE)
         pre = jnp.dot(modded[...], w_ref[0, :, cols], preferred_element_type=F32)
-        hid_ref[1, :, cols] = activation(pre, False).astype(BF16)
-        pol = pre + jnp.dot(low_ref[...], b_ref[:, cols], preferred_element_type=F32)
-        act, slope = activation(pol, True)
-        hid_ref[0, :, cols] = act.astype(BF16)
-        slope_ref[:, cols] = slope
+        pre_ref[1] = pre
+        pre_ref[0] = pre + jnp.dot(low_ref[...], b_ref[:, cols], preferred_element_type=F32)
+
+        @pl.loop(0, CAP * BLK // STRIP)
+        def _(i):
+            strip = pl.ds(pl.multiple_of(i * STRIP, STRIP), STRIP)
+            hid_ref[1, strip, cols] = activation(pre_ref[1, strip, :], False).astype(BF16)
+            act, slope = activation(pre_ref[0, strip, :], True)
+            hid_ref[0, strip, cols] = act.astype(BF16)
+            slope_ref[strip, cols] = slope
 
     def y_core(j):
         src = ypart.at[j, 1 - core]
@@ -641,47 +647,54 @@
         for k in range(1, 8):
             ag_copy(which, k).start()
 
-    _, normed, inverse, _, scale, _ = norm(own, t)
     dl_over().wait_recv()
     dlow = (dlsum[...] + dlrecv[...].astype(F32)).astype(BF16)
     for n in range(4):
         dm_over(n).wait_recv()
-    dm = jnp.concatenate([dmsum[n] + dmrecv[n].astype(F32) for n in range(4)], axis=1)
-    dm = dm + jnp.dot(dlow, at_ref[...], preferred_element_type=F32)
-    dn = dm * scale
-    first = jnp.mean(dn, axis=-1, keepdims=True)
-    second = jnp.mean(dn * normed, axis=-1, keepdims=True)
-    out_grad = cf_ref[pl.ds(t, 1), 0:1] * miss_ref[...]
+    back_ref[...] = jnp.dot(dlow, at_ref[...], preferred_element_type=F32)
+
+    @pl.loop(0, BLK // STRIP)
+    def _(i):
+        strip = pl.ds(pl.multiple_of(i * STRIP, STRIP), STRIP)
+        _, normed, inverse, _, scale, _ = norm(
+            pl.ds(pl.multiple_of(t * BLK + i * STRIP, STRIP), STRIP), t)
+        dm = jnp.concatenate(
+            [dmsum[n, strip, :] + dmrecv[n, strip, :].astype(F32) for n in range(4)], axis=1)
+        dn = (dm + back_ref[strip, :]) * scale
+        first = jnp.mean(dn, axis=-1, keepdims=True)
+        second = jnp.mean(dn * normed, axis=-1, keepdims=True)
+        out_grad = cf_ref[pl.ds(t, 1), 0:1] * miss_ref[strip, :]
+        grad_ref[t, strip, :] = (
+            out_grad + inverse * (dn - first - normed * second)).astype(BF16)
+
+    def tg_copy(which):
+        ref = ga_rows.at[t_y if which == 2 else t]
+        return copy(ref, ref, tg_send.at[which], tg_recv.at[which],
+                    over if which == 1 else mate)
+
+    def tg_arrive(which):
+        ref = ga_rows.at[[t_core, t_y, t_far][which]]
+        copy(ref, ref, tg_send.at[which], tg_recv.at[which], mate).wait_recv()
+
+
+    def g_copy(which):
+        ref = grad_ref.at[t_y] if which == 2 else grad_ref.at[t]
+        return copy(ref, ref, g_send.at[which], g_recv.at[which], over if which == 1 else mate)
+
+    def g_arrive(which):
+        ref = grad_ref.at[[t_core, t_y, t_far][which]]
+        copy(ref, ref, g_send.at[which], g_recv.at[which], mate).wait_recv()
+
+    def g_store(k, block):
+        return pltpu.make_async_copy(
+            grad_ref.at[block], grad_out.at[pl.ds(block * BLK, BLK), :], local.at[7 + k])
+
+    g_copy(1).start()
+    g_copy(0).start()
     for k in range(1, 8):
         ag_arrive(0, k)
     for k in range(8):
         ga_rows[t, :, k * wide:(k + 1) * wide] = ga_ref[t, k]
-
-    def tg_copy(which):
-        ref = ga_rows.at[t_y if which == 2 else t]
-        return copy(ref, ref, tg_send.at[which], tg_recv.at[which],
-                    over if which == 1 else mate)
-
-    def tg_arrive(which):
-        ref = ga_rows.at[[t_core, t_y, t_far][which]]
-        copy(ref, ref, tg_send.at[which], tg_recv.at[which], mate).wait_recv()
-
-    grad_ref[t] = (out_grad + inverse * (dn - first - normed * second)).astype(BF16)
-
-    def g_copy(which):
-        ref = grad_ref.at[t_y] if which == 2 else grad_ref.at[t]
-        return copy(ref, ref, g_send.at[which], g_recv.at[which], over if which == 1 else mate)
-
-    def g_arrive(which):
-        ref = grad_ref.at[[t_core, t_y, t_far][which]]
-        copy(ref, ref, g_send.at[which], g_recv.at[which], mate).wait_recv()
-
-    def g_store(k, block):
-        return pltpu.make_async_copy(
-            grad_ref.at[block], grad_out.at[pl.ds(block * BLK, BLK), :], local.at[7 + k])
-
-    g_copy(1).start()
-    g_copy(0).start()
     tg_copy(1).start()
     tg_copy(0).start()
     g_store(0, t).start()
@@ -772,6 +785,8 @@
             vm((4, 8, 16, width // 8), BF16),
             vm((8, 16, hidden // 2), BF16),
             vm((4, 16, width), BF16),
+            vm((2, rows, TILE), F32),
+            vm((BLK, width), F32),
             dma((11,)),
             vm((2, width, hidden), BF16),
             vm((rows, width), BF16),

time: 146 us -> 145 us (level)
  no operation moved by 1% of the time
where the time goes in v4:
time: 145 us
  Pallas kernels  138 us (95%)
  between operations  3.72 us (3%)
  other arithmetic  2.05 us (1%)
    pallas_call x1, Pallas kernels, fused_device(): pl.pallas_call(step_kernel, out_shape=(jax.ShapeDtypeStruct((1,), F32), j...  138 us

profile of v4, /device:TPU:1, one launch (start us, length us, event | category | flops | bytes accessed | tf_op | source)
XLA Modules:
  0.0 144.8 jit_solution(7015503289555151491)
XLA Ops:
  1.9 138.2 %shard_map.129 = (f32[1]{0:T(128)}, bf16[256,1536]{1,0:T(8,128)(2,1)}, bf16[64,1536]{1,0:T(8,128)(2,1)}, bf16[64,1536]{1,0:T(8,128)(2,1)}) custom-call(s32[1]{0:T(128)S(6)} %copy.16.live_ref, s32[1]{0:T(128)S(6)} %copy.17.wins_ref, s32[1,2]{1,0:T(1,128)} %tail_ref.1, bf16[256,1536]{1,0:T(8,128)(2,1)} %x_hbm.1, bf16[256,1536]{1,0:T(8,128)(2,1)} %t_hbm.1, ...), custom_call_target="tpu_custom_call" | custom-call | tf_op jit(solution)/shard_map/pallas_call | solution.py:765
  140.1 0.0 copy-start
  140.1 2.0 %convert_multiply_fusion = (f32[64,1536]{1,0:T(8,128)}, f32[1536,64]{0,1:T(8,128)}) fusion(bf16[64,1536]{1,0:T(8,128)(2,1)} %get-tuple-element.11, bf16[64,1536]{1,0:T(8,128)(2,1)} %get-tuple-element.10), kind=kLoop, calls=%fused_computation | loop fusion | flops 393216 | bytes 1179648 | tf_op jit(solution)/shard_map/div | solution.py:835
  142.8 0.0 copy-done
  142.8 0.9 copy.19
Async XLA Ops:
  140.1 2.7 %copy-start = (bf16[256,1536]{1,0:T(8,128)(2,1)S(1)}, bf16[256,1536]{1,0:T(8,128)(2,1)}, u32[]{:S(2)}) copy-start(bf16[256,1536]{1,0:T(8,128)(2,1)} %get-tuple-element.19) | copy-start | bytes 2359300
